TPU v7x, 256 devices: a whole 4x4x8 slice. The times are simulated.
256 devices in a mesh: dp: 64 (over x, z, core), outer: 4 (over y).
Axes of the slice: x: 4, y: 4, z: 8, core: 2. Of those that a mesh axis runs over, the one named last changes fastest.
Arguments:
- gradients: bfloat16 [64, 4, 2, 1024, 896], P('dp', 'outer'), may hold values from -48 to 48
- errors: bfloat16 [64, 4, 2, 1024, 896], P('dp', 'outer'), may hold values from -3 to 3
- old_basis: float32 [2, 896, 8], replicated, may hold values from -4 to 4
Outputs:
- new_errors: bfloat16 [64, 4, 2, 1024, 896], P('dp', 'outer')
- new_basis: float32 [2, 896, 8], replicated
All inputs are finite; a program needn't handle non-finite values.
Results may differ from a plain program's by a relative error of at most 0.001.
Values sent between devices are 32-bit elements; how exact they have to be, the bound alone decides.
A program may use at most 64 MiB of HBM per device.

v0:
```python
import jax
import jax.numpy as jnp
from jax import lax
from jax.sharding import PartitionSpec as P

HIGHEST = lax.Precision.HIGHEST
EPSILON = 1e-06


def sum_left(partial_left):
    group_sum = lax.psum(partial_left, "dp")
    return lax.psum(group_sum, "outer")


def sum_right(partial_right):
    group_sum = lax.psum(partial_right, "dp")
    return lax.psum(group_sum, "outer")


def solve_lower(lower_factor, target):
    solved = jax.vmap(
        lambda factor, values: jax.scipy.linalg.solve_triangular(factor, values, lower=True)
    )(lower_factor, jnp.swapaxes(target, 1, 2))
    return jnp.swapaxes(solved, 1, 2)


def compress(grad_part, error_part, basis_part, replicas):
    merged = grad_part.astype(jnp.float32) + error_part.astype(jnp.float32)
    partial_left = jnp.einsum("krc,kcs->krs", merged, basis_part, precision=HIGHEST)
    left_mean = sum_left(partial_left) / replicas
    rank_size = basis_part.shape[2]
    gram_matrix = jnp.einsum("krs,krt->kst", left_mean, left_mean, precision=HIGHEST)
    gram_matrix = gram_matrix + EPSILON * jnp.eye(rank_size, dtype=jnp.float32)
    lower_factor = jnp.linalg.cholesky(gram_matrix)
    orthonormal = solve_lower(lower_factor, left_mean)
    partial_right = jnp.einsum("krc,krs->kcs", merged, orthonormal, precision=HIGHEST)
    new_basis = sum_right(partial_right) / replicas
    update = jnp.einsum("krs,kcs->krc", orthonormal, new_basis, precision=HIGHEST)
    return ((merged - update).astype(jnp.bfloat16), new_basis)


def shards(gradients, errors, old_basis):
    grad_local = gradients[0, 0]
    error_local = errors[0, 0]
    replicas = lax.axis_size("dp") * lax.axis_size("outer")
    pieces = [
        compress(
            grad_local[member : member + 1],
            error_local[member : member + 1],
            old_basis[member : member + 1],
            replicas,
        )
        for member in range(grad_local.shape[0])
    ]
    residual = jnp.concatenate([piece[0] for piece in pieces], axis=0)
    new_basis = jnp.concatenate([piece[1] for piece in pieces], axis=0)
    return (residual[None, None], new_basis)


def solution(mesh):
    in_specs = (P("dp", "outer", None, None, None), P("dp", "outer", None, None, None), P())
    out_specs = (P("dp", "outer", None, None, None), P())
    return jax.shard_map(shards, mesh=mesh, in_specs=in_specs, out_specs=out_specs, check_vma=False)
```

profile of v0, /device:TPU:1, one launch (start us, length us, event | category | flops | bytes accessed | tf_op | source)
XLA Modules:
  0.0 530.8 jit_solution(8338454211307368301)
XLA Ops:
  7.2 0.0 all-reduce.7.cloned.1.call-start
  7.2 6.3 %fusion.23 = f32[1,1024,8]{1,2,0:T(8,128)} fusion(bf16[1,1,2,1024,896]{4,3,2,1,0:T(8,128)(2,1)} %param.7, bf16[1,1,2,1024,896]{4,3,2,1,0:T(8,128)(2,1)} %param.6, f32[2,896,8]{1,2,0:T(8,128)} %param.8), kind=kOutput, calls=%fused_computation.26 | convolution fusion | flops 90832896 | bytes 3731456 | tf_op jit(solution)/shard_map/krc,kcs->krs/dot_general | solution.py:29
  13.5 5.6 %fusion.20 = f32[1,1024,8]{1,2,0:T(8,128)} fusion(bf16[1,1,2,1024,896]{4,3,2,1,0:T(8,128)(2,1)S(1)} %copy-done, bf16[1,1,2,1024,896]{4,3,2,1,0:T(8,128)(2,1)} %param.6, f32[2,896,8]{1,2,0:T(8,128)S(1)} %copy-done.3), kind=kOutput, calls=%fused_computation.25 | convolution fusion | flops 90832896 | bytes 3731456 | tf_op jit(solution)/shard_map/krc,kcs->krs/dot_general | solution.py:29
  19.1 0.0 all-reduce.7.cloned.1.call-update
  19.2 0.0 all-reduce.9.cloned.1.call-start
  19.2 172.2 %all-reduce.7.cloned.1.call-done = (f32[1,1024,8]{1,2,0:T(8,128)}, f32[1,1024,8]{1,2,0:T(8,128)}) async-done(((f32[1,1024,8]{1,2,0:T(8,128)}, f32[1,1024,8]{1,2,0:T(8,128)}), (f32[1,1024,8]{1,2,0:T(8,128)}, f32[1,1024,8]{1,2,0:T(8,128)})) %all-reduce.7.cloned.1.call-update) | async-done | bytes 65552 | tf_op jit(solution)/shard_map/psum | solution.py:11
  191.4 0.0 all-reduce.9.cloned.1.call-update
  191.4 43.2 %all-reduce.9.cloned.1.call-done = (f32[1,1024,8]{1,2,0:T(8,128)}, f32[1,1024,8]{1,2,0:T(8,128)}) async-done(((f32[1,1024,8]{1,2,0:T(8,128)}, f32[1,1024,8]{1,2,0:T(8,128)}), (f32[1,1024,8]{1,2,0:T(8,128)}, f32[1,1024,8]{1,2,0:T(8,128)})) %all-reduce.9.cloned.1.call-update) | async-done | bytes 65552 | tf_op jit(solution)/shard_map/psum | solution.py:12
  234.6 1.0 fusion.32
  235.6 1.0 fusion.33
  236.7 0.1 copy.5
  236.7 0.7 custom-call.8
  237.4 0.1 select_reduce_fusion.1
  237.5 0.6 compare_reduce_fusion.1
  238.1 0.6 fusion.54
  238.8 0.6 custom-call.9
  239.4 1.0 fusion.36
  240.4 0.1 copy.7
  240.5 0.7 custom-call.10
  241.2 0.1 select_reduce_fusion
  241.3 0.6 compare_reduce_fusion
  241.9 0.6 fusion.55
  242.6 0.6 custom-call.11
  243.2 1.1 fusion.34
  244.3 4.3 fusion.29
  248.7 3.8 fusion.26
  252.5 246.1 %all-reduce = (f32[1,896,8]{1,2,0:T(8,128)S(1)}, f32[1,896,8]{1,2,0:T(8,128)S(1)}) all-reduce(f32[1,896,8]{1,2,0:T(8,128)S(1)} %fusion.29, f32[1,896,8]{1,2,0:T(8,128)S(1)} %fusion.26), channel_id=1, replica_groups=mesh['dp'=64,'outer'=4] {'dp'}, use_global_device_ids=true, to_apply=%region_8.11 | all-reduce | flops 14336 | bytes 114688 | tf_op jit(solution)/shard_map/psum | solution.py:16
  498.5 12.9 %all-reduce.2 = (f32[1,896,8]{1,2,0:T(8,128)S(1)}, f32[1,896,8]{1,2,0:T(8,128)S(1)}) all-reduce(f32[1,896,8]{1,2,0:T(8,128)S(1)} %get-tuple-element.4, f32[1,896,8]{1,2,0:T(8,128)S(1)} %get-tuple-element.5), channel_id=1, replica_groups=mesh['dp'=64,'outer'=4] {'outer'}, use_global_device_ids=true, to_apply=%region_9.12 | all-reduce | flops 14336 | bytes 114688 | tf_op jit(solution)/shard_map/psum | solution.py:17
  511.4 5.0 fusion.10
  516.5 4.7 fusion.11
  521.2 0.6 pad_maximum_fusion
  521.8 2.2 maximum_bitcast_fusion
  (11 shorter events, 0.0 us)
Async XLA Ops:
  7.2 6.4 %copy-start.3 = (f32[2,896,8]{1,2,0:T(8,128)S(1)}, f32[2,896,8]{1,2,0:T(8,128)}, u32[]{:S(2)}) copy-start(f32[2,896,8]{1,2,0:T(8,128)} %param.8) | copy-start | bytes 172036
  7.2 184.2 %all-reduce.7.cloned.1.call-start = ((), (), s32[]{:S(2)}) async-start(), calls=%async_computation | async-start | bytes 131072 | tf_op jit(solution)/shard_map/psum | solution.py:11
  7.2 6.3 %copy-start = (bf16[1,1,2,1024,896]{4,3,2,1,0:T(8,128)(2,1)S(1)}, bf16[1,1,2,1024,896]{4,3,2,1,0:T(8,128)(2,1)}, u32[]{:S(2)}) copy-start(bf16[1,1,2,1024,896]{4,3,2,1,0:T(8,128)(2,1)} %param.7) | copy-start | bytes 11010052
  19.2 215.5 %all-reduce.9.cloned.1.call-start = ((), (), s32[]{:S(2)}) async-start(), calls=%async_computation.1 | async-start | bytes 131072 | tf_op jit(solution)/shard_map/psum | solution.py:12
  243.2 5.5 %copy-start.1 = (bf16[1,1,2,1024,896]{4,3,2,1,0:T(8,128)(2,1)S(1)}, bf16[1,1,2,1024,896]{4,3,2,1,0:T(8,128)(2,1)}, u32[]{:S(2)}) copy-start(bf16[1,1,2,1024,896]{4,3,2,1,0:T(8,128)(2,1)} %param.7) | copy-start | bytes 11010052
  511.4 5.1 copy-start.2
Sparse Core Ops, SparseCore 0:
  19.3 172.0 all-reduce.6
  193.8 40.8 all-reduce.8
where the time goes:
time: 537 us; the launch traced here: 531 us
  blocking collectives  259 us (48%)
  waiting for transfers between devices  215 us (40%)
  matrix products  33.9 us (6%)
  between operations  14.2 us (3%)
  other arithmetic  8.2 us (2%)
    psum x1, blocking collectives, sum_right(): group_sum = lax.psum(partial_right, 'dp')  246 us
    psum x1, waiting for transfers between devices, sum_left(): group_sum = lax.psum(partial_left, 'dp')  172 us
    psum x1, waiting for transfers between devices, sum_left(): return lax.psum(group_sum, 'outer')  43.2 us
    psum x1, blocking collectives, sum_right(): return lax.psum(group_sum, 'outer')  12.9 us
    dot_general x2, matrix products, compress(): jnp.einsum('krc,kcs->krs', merged, basis_part, precision=HIGHEST)  11.9 us
  transfers between devices with their start and end apart: 2, of which 2 were waited for; matrix products, arithmetic and copies ran while one was open for 0% of the time, Pallas kernels for 0%

commit v1 on v0

v1 whole, which is shorter than its diff:
```python
import functools
import itertools

import jax
import jax.numpy as jnp
from jax import lax
from jax.experimental import pallas as pl
from jax.experimental.pallas import tpu as pltpu
from jax.sharding import PartitionSpec as P

MESH = pl.DeviceIdType.MESH
HIGHEST = lax.Precision.HIGHEST
EPSILON = 1e-06
NX, NY, NZ, NC = 4, 4, 8, 2
PLANE = NX * NY * NC
REPLICAS = PLANE * NZ
BLOCK = 256


def ring(d, n):
    return min(d % n, n - d % n)


PLANE_OFFSETS = sorted(
    (o for o in itertools.product(range(NX), range(NY), range(NC)) if any(o)),
    key=lambda o: -(ring(o[0], NX) + ring(o[1], NY) + 0.5 * o[2]),
)
Z_OFFSETS = sorted(range(1, NZ), key=lambda d: -ring(d, NZ))


def split3(value):
    high = value.astype(jnp.bfloat16).astype(jnp.float32)
    rest = value - high
    middle = rest.astype(jnp.bfloat16).astype(jnp.float32)
    return high, middle, rest - middle


def stacked(value):
    return jnp.concatenate(split3(value), axis=0).astype(jnp.bfloat16)


def fold(product):
    return product[0:8] + product[8:16] + product[16:24]


def reduce_kernel(
    g_hbm, e_hbm, q_hbm,
    gv, ev, factors, basis,
    qv, send1, slot1, part1, zslot1, final1, gather1,
    send2, slot2, part2, zslot2, final2, gather2,
    in_sem, q_sem, send_sem, recv_sem,
):
    matrices, rows, cols = gv.shape
    per = rows // BLOCK
    dp, y = lax.axis_index("dp"), lax.axis_index("outer")
    x, z, c = lax.div(dp, NZ * NC), lax.rem(lax.div(dp, NC), NZ), lax.rem(dp, NC)
    mine = (x * NY + y) * NC + c

    q_copy = pltpu.make_async_copy(q_hbm, qv, q_sem)
    q_copy.start()
    loads = []
    for m in range(matrices):
        for i in range(per):
            at = pl.ds(i * BLOCK, BLOCK)
            pair = []
            for a, (src, dst) in enumerate(((g_hbm, gv), (e_hbm, ev))):
                copy = pltpu.make_async_copy(src.at[m, at], dst.at[m, at], in_sem.at[m, i, a])
                copy.start()
                pair.append(copy)
            loads.append((m, i, pair))

    plane = []
    for dx, dy, dc in PLANE_OFFSETS:
        tx, ty, tc = lax.rem(x + dx, NX), lax.rem(y + dy, NY), lax.rem(c + dc, NC)
        plane.append(((tx * NY + ty) * NC + tc, {"dp": (tx * NZ + z) * NC + tc, "outer": ty}))
    column = [{"dp": (x * NZ + lax.rem(z + d, NZ)) * NC + c, "outer": y} for d in Z_OFFSETS]
    barrier = pltpu.get_barrier_semaphore()
    for device in [d for _, d in plane] + column:
        pl.semaphore_signal(barrier, inc=1, device_id=device, device_id_type=MESH)

    def wait_all(ref, sem):
        pltpu.make_async_copy(ref, ref, sem).wait()

    def remote(src, dst, k, device):
        pltpu.make_async_remote_copy(
            src_ref=src, dst_ref=dst, send_sem=send_sem.at[k], recv_sem=recv_sem.at[k],
            device_id=device, device_id_type=MESH,
        ).start()

    def scatter(send, slot, k):
        for index, device in plane:
            remote(send.at[index], slot.at[mine], k, device)
        pltpu.make_async_copy(send.at[mine], slot.at[mine], recv_sem.at[k]).start()

    def exchange(slot, part, zslot, k):
        wait_all(slot, recv_sem.at[k])
        total = slot[0]
        for i in range(1, PLANE):
            total = total + slot[i]
        part[...] = total
        for device in column:
            remote(part, zslot.at[z], k + 1, device)
        pltpu.make_async_copy(part, zslot.at[z], recv_sem.at[k + 1]).start()

    def spread(zslot, final, gather, k):
        wait_all(zslot, recv_sem.at[k + 1])
        total = zslot[0]
        for i in range(1, NZ):
            total = total + zslot[i]
        final[...] = total * (1.0 / REPLICAS)
        for _, device in plane:
            remote(final, gather.at[mine], k + 2, device)
        pltpu.make_async_copy(final, gather.at[mine], recv_sem.at[k + 2]).start()

    def assembled(gather, m, blocks):
        tiles = [
            jnp.concatenate([gather[m * 16 + b], gather[m * 16 + 8 + b]], axis=0) for b in range(blocks)
        ]
        return jnp.concatenate(tiles, axis=1)

    def place(send, m, b, tile):
        send[m * 16 + b] = tile[0:4]
        send[m * 16 + 8 + b] = tile[4:8]

    q_copy.wait()
    q_terms = [stacked(qv[m]) for m in range(matrices)]
    contract_last = (((1,), (1,)), ((), ()))
    for m, i, pair in loads:
        for copy in pair:
            copy.wait()
        at = pl.ds(i * BLOCK, BLOCK)
        left = fold(
            lax.dot_general(q_terms[m], gv[m, at], contract_last, preferred_element_type=jnp.float32)
            + lax.dot_general(q_terms[m], ev[m, at], contract_last, preferred_element_type=jnp.float32)
        )
        for b in range(BLOCK // 128):
            place(send1, m, i * (BLOCK // 128) + b, left[:, b * 128 : (b + 1) * 128])

    pl.semaphore_wait(barrier, len(plane) + len(column))
    scatter(send1, slot1, 0)
    exchange(slot1, part1, zslot1, 0)
    spread(zslot1, final1, gather1, 0)
    wait_all(gather1, recv_sem.at[2])

    left_mean = [assembled(gather1, m, rows // 128) for m in range(matrices)]
    for m in range(matrices):
        terms = stacked(left_mean[m])
        right = fold(
            jnp.dot(terms, gv[m], preferred_element_type=jnp.float32)
            + jnp.dot(terms, ev[m], preferred_element_type=jnp.float32)
        )
        for b in range(cols // 128):
            place(send2, m, b, right[:, b * 128 : (b + 1) * 128])
        for b in range(cols // 128, 8):
            place(send2, m, b, jnp.zeros((8, 128), jnp.float32))
    scatter(send2, slot2, 3)

    row_of = lax.broadcasted_iota(jnp.int32, (8, 1), 0)
    eye = (
        lax.broadcasted_iota(jnp.int32, (8, 8), 0) == lax.broadcasted_iota(jnp.int32, (8, 8), 1)
    ).astype(jnp.float32)
    inverses = []
    for m in range(matrices):
        gram = lax.dot_general(
            left_mean[m], left_mean[m], contract_last, precision=HIGHEST, preferred_element_type=jnp.float32
        )
        gram = gram + EPSILON * eye
        inverse, solved = eye, left_mean[m]
        for k in range(8):
            pivot = jnp.sqrt(gram[k : k + 1, k : k + 1])
            across = gram[k : k + 1, :] / pivot
            below = jnp.where(row_of > k, gram[:, k : k + 1] / pivot, 0.0)
            gram = gram - below * across
            first = inverse[k : k + 1, :] / pivot
            inverse = jnp.where(row_of == k, first, inverse - below * first)
            first = solved[k : k + 1, :] / pivot
            solved = jnp.where(row_of == k, first, solved - below * first)
        inverses.append(inverse)
        o1, o2, o3 = split3(solved)
        wide = jnp.concatenate([o1, o1, o2, o2, o1, o3, jnp.zeros((80, rows), jnp.float32)], axis=0)
        factors[m] = jnp.transpose(wide).astype(jnp.bfloat16)

    exchange(slot2, part2, zslot2, 3)
    spread(zslot2, final2, gather2, 3)
    wait_all(gather2, recv_sem.at[5])
    for m in range(matrices):
        raw = assembled(gather2, m, cols // 128)
        total = inverses[m][:, 0:1] * raw[0:1, :]
        for t in range(1, 8):
            total = total + inverses[m][:, t : t + 1] * raw[t : t + 1, :]
        basis[m] = total

    for k in (0, 3):
        wait_all(slot1.at[pl.ds(0, PLANE - 1)], send_sem.at[k])
        wait_all(zslot1.at[pl.ds(0, NZ - 1)], send_sem.at[k + 1])
        wait_all(gather1.at[pl.ds(0, PLANE - 1)], send_sem.at[k + 2])


def residual_kernel(gv, ev, factors, basis, out_hbm, basis_hbm, buffer, out_sem, basis_sem):
    matrices, rows, cols = gv.shape
    basis_copy = pltpu.make_async_copy(basis, basis_hbm, basis_sem)
    basis_copy.start()
    for m in range(matrices):
        b1, b2, b3 = split3(basis[m])
        terms = jnp.concatenate(
            [b1, b2, b1, b2, b3, b1, jnp.zeros((80, cols), jnp.float32)], axis=0
        ).astype(jnp.bfloat16)
        for i in range(rows // BLOCK):
            at = pl.ds(i * BLOCK, BLOCK)
            update = jnp.dot(factors[m, at], terms, preferred_element_type=jnp.float32)
            merged = gv[m, at].astype(jnp.float32) + ev[m, at].astype(jnp.float32)
            buffer[m, at] = (merged - update).astype(jnp.bfloat16)
            pltpu.make_async_copy(buffer.at[m, at], out_hbm.at[m, at], out_sem).start()
    pltpu.make_async_copy(buffer, out_hbm, out_sem).wait()
    basis_copy.wait()


def shards(gradients, errors, old_basis):
    _, _, matrices, rows, cols = gradients.shape
    rank = old_basis.shape[2]
    any_space = pl.BlockSpec(memory_space=pl.ANY)
    vmem = pl.BlockSpec(memory_space=pltpu.VMEM)
    f32 = jnp.float32
    stage = [
        pltpu.VMEM((PLANE, 4, 128), f32),
        pltpu.VMEM((PLANE, 4, 128), f32),
        pltpu.VMEM((4, 128), f32),
        pltpu.VMEM((NZ, 4, 128), f32),
        pltpu.VMEM((4, 128), f32),
        pltpu.VMEM((PLANE, 4, 128), f32),
    ]
    gv, ev, factors, basis = pl.pallas_call(
        reduce_kernel,
        out_shape=(
            pltpu.VMEM((matrices, rows, cols), jnp.bfloat16),
            pltpu.VMEM((matrices, rows, cols), jnp.bfloat16),
            pltpu.VMEM((matrices, rows, 128), jnp.bfloat16),
            pltpu.VMEM((matrices, rank, cols), f32),
        ),
        in_specs=[pl.BlockSpec(memory_space=pltpu.HBM)] * 3,
        out_specs=(vmem,) * 4,
        scratch_shapes=[pltpu.VMEM((matrices, rank, cols), f32)]
        + stage
        + stage
        + [
            pltpu.SemaphoreType.DMA((matrices, rows // BLOCK, 2)),
            pltpu.SemaphoreType.DMA,
            pltpu.SemaphoreType.DMA((6,)),
            pltpu.SemaphoreType.DMA((6,)),
        ],
        compiler_params=pltpu.CompilerParams(
            collective_id=0, has_side_effects=True, vmem_limit_bytes=24 << 20
        ),
        name="reduce",
    )(gradients[0, 0], errors[0, 0], jnp.swapaxes(old_basis, 1, 2))
    residual, new_basis = pl.pallas_call(
        residual_kernel,
        out_shape=(
            jax.ShapeDtypeStruct((matrices, rows, cols), jnp.bfloat16),
            jax.ShapeDtypeStruct((matrices, rank, cols), f32),
        ),
        in_specs=[vmem] * 4,
        out_specs=(any_space,) * 2,
        scratch_shapes=[
            pltpu.VMEM((matrices, rows, cols), jnp.bfloat16),
            pltpu.SemaphoreType.DMA,
            pltpu.SemaphoreType.DMA,
        ],
        compiler_params=pltpu.CompilerParams(vmem_limit_bytes=24 << 20),
        name="residual",
    )(gv, ev, factors, basis)
    return residual[None, None], jnp.swapaxes(new_basis, 1, 2)


def solution(mesh):
    in_specs = (P("dp", "outer", None, None, None), P("dp", "outer", None, None, None), P())
    out_specs = (P("dp", "outer", None, None, None), P())
    return jax.shard_map(shards, mesh=mesh, in_specs=in_specs, out_specs=out_specs, check_vma=False)
```

time: 537 us -> 52.7 us (0.10); the launches traced: 531 us -> 52.5 us
  blocking collectives: 259 us -> 0 us
  waiting for transfers between devices: 215 us -> 0 us
  Pallas kernels: 0 us -> 47 us
  matrix products: 33.9 us -> 0 us
  between operations: 14.2 us -> 0.65 us
  other arithmetic: 8.2 us -> 0 us
    psum x2 -> x0, blocking collectives: 259 us -> none  [the longest x1 246 us: sum_right(): group_sum = lax.psum(partial_right, 'dp')]
    psum x2 -> x0, waiting for transfers between devices: 215 us -> none  [the longest x1 172 us: sum_left(): group_sum = lax.psum(partial_left, 'dp')]
    pallas_call x0 -> x2, Pallas kernels: none -> 47 us  [the longest x1 44.8 us: shards(): pl.pallas_call(reduce_kernel, out_shape=(pltpu.VMEM((matrices, rows, cols...]
    dot_general x8 -> x0, matrix products: 31.8 us -> none  [the longest x2 11.9 us: compress(): jnp.einsum('krc,kcs->krs', merged, basis_part, precision=HIGHEST)]
  transfers between devices with their start and end apart: 2 -> 0, of which waited for: 2 -> 0; matrix products, arithmetic and copies ran while one was open for 0% -> 0% of each run, Pallas kernels for 0% -> 0%
where the time goes in v1:
time: 52.7 us; the launch traced here: 52.5 us
  Pallas kernels  47 us (89%)
  local copies, waits for them, and re-layouts  4.89 us (9%)
  between operations  0.65 us (1%)
    pallas_call x1, Pallas kernels, shards(): pl.pallas_call(reduce_kernel, out_shape=(pltpu.VMEM((matrices, rows, cols...  44.8 us
    unnamed x6, local copies, waits for them, and re-layouts  4.89 us
    pallas_call x1, Pallas kernels, shards(): pl.pallas_call(residual_kernel, out_shape=(jax.ShapeDtypeStruct((matrices...  2.16 us

profile of v1, /device:TPU:1, one launch (start us, length us, event | category | flops | bytes accessed | tf_op | source)
XLA Modules:
  0.0 52.5 jit_solution(4050560370621518635)
XLA Ops:
  0.6 0.0 copy-start
  0.6 2.0 %copy-done = bf16[1,1,2,1024,896]{4,3,2,1,0:T(8,128)(2,1)S(1)} copy-done((bf16[1,1,2,1024,896]{4,3,2,1,0:T(8,128)(2,1)S(1)}, bf16[1,1,2,1024,896]{4,3,2,1,0:T(8,128)(2,1)}, u32[]{:S(2)}) %copy-start) | copy-done | bytes 3670040
  2.7 0.0 copy-start.1
  2.7 2.0 %copy-done.1 = bf16[1,1,2,1024,896]{4,3,2,1,0:T(8,128)(2,1)S(1)} copy-done((bf16[1,1,2,1024,896]{4,3,2,1,0:T(8,128)(2,1)S(1)}, bf16[1,1,2,1024,896]{4,3,2,1,0:T(8,128)(2,1)}, u32[]{:S(2)}) %copy-start.1) | copy-done | bytes 3670040
  4.7 0.0 copy-start.2
  4.7 0.8 %copy-done.2 = f32[2,896,8]{1,2,0:T(8,128)S(1)} copy-done((f32[2,896,8]{1,2,0:T(8,128)S(1)}, f32[2,896,8]{1,2,0:T(8,128)}, u32[]{:S(2)}) %copy-start.2) | copy-done | bytes 57368
  5.5 44.8 %reduce.1 = (bf16[2,1024,896]{2,1,0:T(8,128)(2,1)S(1)}, bf16[2,1024,896]{2,1,0:T(8,128)(2,1)S(1)}, bf16[2,1024,128]{2,1,0:T(8,128)(2,1)S(1)}, f32[2,8,896]{2,1,0:T(8,128)S(1)}) custom-call(bf16[2,1024,896]{2,1,0:T(8,128)(2,1)S(1)} %bitcast.5, bf16[2,1024,896]{2,1,0:T(8,128)(2,1)S(1)} %bitcast.6, f32[2,8,896]{2,1,0:T(8,128)S(1)} %bitcast.7), custom_call_target="tpu_custom_call" | custom-call | tf_op jit(solution)/shard_map/reduce/pallas_call | solution.py:232
  50.4 2.2 %residual.1 = (bf16[2,1024,896]{2,1,0:T(8,128)(2,1)}, f32[2,8,896]{2,1,0:T(8,128)}) custom-call(bf16[2,1024,896]{2,1,0:T(8,128)(2,1)S(1)} %get-tuple-element.8.gv, bf16[2,1024,896]{2,1,0:T(8,128)(2,1)S(1)} %get-tuple-element.9.ev, bf16[2,1024,128]{2,1,0:T(8,128)(2,1)S(1)} %get-tuple-element.10.factors, f32[2,8,896]{2,1,0:T(8,128)S(1)} %get-tuple-element.11.basis), custom_call_target="tpu_custom_call" | custom-call | tf_op jit(solution)/shard_map/residual/pallas_call | solution.py:256
Async XLA Ops:
  0.6 2.0 %copy-start = (bf16[1,1,2,1024,896]{4,3,2,1,0:T(8,128)(2,1)S(1)}, bf16[1,1,2,1024,896]{4,3,2,1,0:T(8,128)(2,1)}, u32[]{:S(2)}) copy-start(bf16[1,1,2,1024,896]{4,3,2,1,0:T(8,128)(2,1)} %param.3) | copy-start | bytes 11010052
  2.7 2.0 %copy-start.1 = (bf16[1,1,2,1024,896]{4,3,2,1,0:T(8,128)(2,1)S(1)}, bf16[1,1,2,1024,896]{4,3,2,1,0:T(8,128)(2,1)}, u32[]{:S(2)}) copy-start(bf16[1,1,2,1024,896]{4,3,2,1,0:T(8,128)(2,1)} %param.4) | copy-start | bytes 11010052
  4.7 0.8 %copy-start.2 = (f32[2,896,8]{1,2,0:T(8,128)S(1)}, f32[2,896,8]{1,2,0:T(8,128)}, u32[]{:S(2)}) copy-start(f32[2,896,8]{1,2,0:T(8,128)} %param.5) | copy-start | bytes 172036

commit v2 on v1

v2 whole, which is shorter than its diff:
```python
import functools
import itertools

import jax
import jax.numpy as jnp
from jax import lax
from jax.experimental import pallas as pl
from jax.experimental.pallas import tpu as pltpu
from jax.sharding import PartitionSpec as P

MESH = pl.DeviceIdType.MESH
HIGHEST = lax.Precision.HIGHEST
EPSILON = 1e-06
NX, NY, NZ, NC = 4, 4, 8, 2
PLANE = NX * NY * NC
REPLICAS = PLANE * NZ
BLOCK = 256
LOAD = 512
FAR = 5


def ring(d, n):
    return min(d % n, n - d % n)


XY_OFFSETS = sorted(itertools.product(range(NX), range(NY)), key=lambda o: -(ring(o[0], NX) + ring(o[1], NY)))
Z_OFFSETS = sorted(range(1, NZ), key=lambda d: -ring(d, NZ))


def split3(value):
    high = value.astype(jnp.bfloat16).astype(jnp.float32)
    rest = value - high
    middle = rest.astype(jnp.bfloat16).astype(jnp.float32)
    return high, middle, rest - middle


def stacked(value):
    return jnp.concatenate(split3(value), axis=0).astype(jnp.bfloat16)


def tree_sum(terms):
    while len(terms) > 1:
        terms = [a + b for a, b in zip(terms[::2], terms[1::2])]
    return terms[0]


def fold(product):
    return product[0:8] + product[8:16] + product[16:24]


def reduce_kernel(
    g_hbm, e_hbm, q_hbm,
    merged, factors, basis,
    gv, ev, qv, send1, slot1, part1, zslot1, final1, gather1,
    send2, slot2, part2, zslot2, final2, gather2,
    in_sem, q_sem, send_sem, recv_sem,
):
    _, rows, cols = gv.shape
    per = rows // LOAD
    dp, y = lax.axis_index("dp"), lax.axis_index("outer")
    x, z, c = lax.div(dp, NZ * NC), lax.rem(lax.div(dp, NC), NZ), lax.rem(dp, NC)
    own, other = c, 1 - c
    place_xy = x * NY + y
    sender = place_xy * NC + c

    here, across = [], []
    for dx, dy in XY_OFFSETS:
        tx, ty = lax.rem(x + dx, NX), lax.rem(y + dy, NY)
        index = tx * NY + ty
        if dx or dy:
            here.append((index, {"dp": (tx * NZ + z) * NC + own, "outer": ty}))
        across.append((index, {"dp": (tx * NZ + z) * NC + other, "outer": ty}))
    column = [{"dp": (x * NZ + lax.rem(z + d, NZ)) * NC + c, "outer": y} for d in Z_OFFSETS]
    partners = [d for _, d in across[:4]] + column[:3] + [d for _, d in here + across[4:]] + column[3:]
    barrier = pltpu.get_barrier_semaphore()
    for device in partners:
        pl.semaphore_signal(barrier, inc=1, device_id=device, device_id_type=MESH)

    q_copy = pltpu.make_async_copy(q_hbm, qv, q_sem)
    q_copy.start()
    loads = []
    for n, m in enumerate((other, own)):
        for i in range(per):
            at = pl.ds(i * LOAD, LOAD)
            pair = []
            for a, (src, dst) in enumerate(((g_hbm, gv), (e_hbm, ev))):
                copy = pltpu.make_async_copy(src.at[m, at], dst.at[m, at], in_sem.at[n, i, a])
                copy.start(priority=n)
                pair.append(copy)
            loads.append((n, m, i, pair))

    def wait_all(ref, sem):
        pltpu.make_async_copy(ref, ref, sem).wait()

    def remote(src, dst, send, recv, device):
        pltpu.make_async_remote_copy(
            src_ref=src, dst_ref=dst, send_sem=send_sem.at[send], recv_sem=recv_sem.at[recv],
            device_id=device, device_id_type=MESH,
        ).start()

    def scatter_across(send, m, slot, k):
        for index, device in across:
            remote(send.at[m, index], slot.at[sender], k, k, device)

    def scatter_here(send, m, slot, k):
        for index, device in here:
            remote(send.at[m, index], slot.at[sender], k, k, device)
        pltpu.make_async_copy(send.at[m, place_xy], slot.at[sender], recv_sem.at[k]).start()

    def exchange(slot, part, zslot, k):
        wait_all(slot, recv_sem.at[k])
        part[...] = tree_sum([slot[i] for i in range(PLANE)])
        for device in column:
            remote(part, zslot.at[z], k + 1, k + 1, device)
        pltpu.make_async_copy(part, zslot.at[z], recv_sem.at[k + 1]).start()

    def spread(zslot, final, gather, m, k):
        wait_all(zslot, recv_sem.at[k + 1])
        final[...] = tree_sum([zslot[i] for i in range(NZ)]) * (1.0 / REPLICAS)
        for _, device in here[:FAR]:
            remote(final, gather.at[m, place_xy], k + 2, k + 2, device)
        for _, device in across:
            remote(final, gather.at[m, place_xy], k + 2, k + 3, device)
        for _, device in here[FAR:]:
            remote(final, gather.at[m, place_xy], k + 2, k + 2, device)
        pltpu.make_async_copy(final, gather.at[m, place_xy], recv_sem.at[k + 2]).start()

    def assembled(gather, m, blocks):
        tiles = [jnp.concatenate([gather[m, b], gather[m, 8 + b]], axis=0) for b in range(blocks)]
        return jnp.concatenate(tiles, axis=1)

    def place(send, m, b, tile):
        send[m, b] = tile[0:4]
        send[m, 8 + b] = tile[4:8]

    contract_last = (((1,), (1,)), ((), ()))
    q_copy.wait()
    q_terms = [stacked(qv[m]) for m in (other, own)]
    for n, m, i, pair in loads:
        for copy in pair:
            copy.wait()
        at = pl.ds(i * LOAD, LOAD)
        left = fold(
            lax.dot_general(q_terms[n], gv[m, at], contract_last, preferred_element_type=jnp.float32)
            + lax.dot_general(q_terms[n], ev[m, at], contract_last, preferred_element_type=jnp.float32)
        )
        for b in range(LOAD // 128):
            place(send1, m, i * (LOAD // 128) + b, left[:, b * 128 : (b + 1) * 128])
        if n == 1 and i == per - 2:
            pl.semaphore_wait(barrier, len(partners))
            scatter_across(send1, other, slot1, 0)
    scatter_here(send1, own, slot1, 0)
    for n in range(2):
        for i in range(rows // BLOCK):
            at = pl.ds(i * BLOCK, BLOCK)
            merged[n, at] = gv[n, at].astype(jnp.float32) + ev[n, at].astype(jnp.float32)
    exchange(slot1, part1, zslot1, 0)
    spread(zslot1, final1, gather1, own, 0)

    def right(m):
        mean = assembled(gather1, m, rows // 128)
        terms = stacked(mean)
        product = fold(
            jnp.dot(terms, gv[m], preferred_element_type=jnp.float32)
            + jnp.dot(terms, ev[m], preferred_element_type=jnp.float32)
        )
        for b in range(cols // 128):
            place(send2, m, b, product[:, b * 128 : (b + 1) * 128])
        for b in range(cols // 128, 8):
            place(send2, m, b, jnp.zeros((8, 128), jnp.float32))
        return mean

    wait_all(gather1.at[own], recv_sem.at[2])
    mean_own = right(own)
    scatter_across(send2, own, slot2, 4)
    wait_all(gather1.at[other], recv_sem.at[3])
    mean_other = right(other)
    scatter_here(send2, other, slot2, 4)

    row_of = lax.broadcasted_iota(jnp.int32, (8, 1), 0)
    eye = (
        lax.broadcasted_iota(jnp.int32, (8, 8), 0) == lax.broadcasted_iota(jnp.int32, (8, 8), 1)
    ).astype(jnp.float32)
    inverses = []
    for m, mean in ((own, mean_own), (other, mean_other)):
        gram = lax.dot_general(mean, mean, contract_last, precision=HIGHEST, preferred_element_type=jnp.float32)
        gram = gram + EPSILON * eye
        inverse, solved = eye, mean
        for k in range(8):
            pivot = jnp.sqrt(gram[k : k + 1, k : k + 1])
            across_row = gram[k : k + 1, :] / pivot
            below = jnp.where(row_of > k, gram[:, k : k + 1] / pivot, 0.0)
            gram = gram - below * across_row
            first = inverse[k : k + 1, :] / pivot
            inverse = jnp.where(row_of == k, first, inverse - below * first)
            first = solved[k : k + 1, :] / pivot
            solved = jnp.where(row_of == k, first, solved - below * first)
        inverses.append((m, inverse))
        o1, o2, o3 = split3(solved)
        wide = jnp.concatenate([o1, o1, o2, o2, o1, o3, jnp.zeros((80, rows), jnp.float32)], axis=0)
        factors[m] = jnp.transpose(wide).astype(jnp.bfloat16)

    exchange(slot2, part2, zslot2, 4)
    spread(zslot2, final2, gather2, other, 4)
    wait_all(gather2.at[other], recv_sem.at[6])
    wait_all(gather2.at[own], recv_sem.at[7])
    for m, inverse in inverses:
        raw = assembled(gather2, m, cols // 128)
        basis[m] = tree_sum([inverse[:, t : t + 1] * raw[t : t + 1, :] for t in range(8)])

    for k in (0, 4):
        wait_all(slot1.at[pl.ds(0, PLANE - 1)], send_sem.at[k])
        wait_all(zslot1.at[pl.ds(0, NZ - 1)], send_sem.at[k + 1])
        wait_all(slot1.at[pl.ds(0, PLANE - 1)], send_sem.at[k + 2])


def residual_kernel(merged, factors, basis, out_hbm, basis_hbm, buffer, out_sem, basis_sem):
    matrices, rows, cols = merged.shape
    basis_copy = pltpu.make_async_copy(basis, basis_hbm, basis_sem)
    basis_copy.start()
    for m in range(matrices):
        b1, b2, b3 = split3(basis[m])
        terms = jnp.concatenate(
            [b1, b2, b1, b2, b3, b1, jnp.zeros((80, cols), jnp.float32)], axis=0
        ).astype(jnp.bfloat16)
        for i in range(rows // BLOCK):
            at = pl.ds(i * BLOCK, BLOCK)
            update = jnp.dot(factors[m, at], terms, preferred_element_type=jnp.float32)
            buffer[m, at] = (merged[m, at] - update).astype(jnp.bfloat16)
            pltpu.make_async_copy(buffer.at[m, at], out_hbm.at[m, at], out_sem).start()
    pltpu.make_async_copy(buffer, out_hbm, out_sem).wait()
    basis_copy.wait()


def shards(gradients, errors, old_basis):
    _, _, matrices, rows, cols = gradients.shape
    rank = old_basis.shape[2]
    any_space = pl.BlockSpec(memory_space=pl.ANY)
    vmem = pl.BlockSpec(memory_space=pltpu.VMEM)
    f32 = jnp.float32
    stage = [
        pltpu.VMEM((matrices, 16, 4, 128), f32),
        pltpu.VMEM((PLANE, 4, 128), f32),
        pltpu.VMEM((4, 128), f32),
        pltpu.VMEM((NZ, 4, 128), f32),
        pltpu.VMEM((4, 128), f32),
        pltpu.VMEM((matrices, 16, 4, 128), f32),
    ]
    merged, factors, basis = pl.pallas_call(
        reduce_kernel,
        out_shape=(
            pltpu.VMEM((matrices, rows, cols), f32),
            pltpu.VMEM((matrices, rows, 128), jnp.bfloat16),
            pltpu.VMEM((matrices, rank, cols), f32),
        ),
        in_specs=[pl.BlockSpec(memory_space=pltpu.HBM)] * 3,
        out_specs=(vmem,) * 3,
        scratch_shapes=[
            pltpu.VMEM((matrices, rows, cols), jnp.bfloat16),
            pltpu.VMEM((matrices, rows, cols), jnp.bfloat16),
            pltpu.VMEM((matrices, rank, cols), f32),
        ]
        + stage
        + stage
        + [
            pltpu.SemaphoreType.DMA((matrices, rows // LOAD, 2)),
            pltpu.SemaphoreType.DMA,
            pltpu.SemaphoreType.DMA((8,)),
            pltpu.SemaphoreType.DMA((8,)),
        ],
        compiler_params=pltpu.CompilerParams(
            collective_id=0, has_side_effects=True, vmem_limit_bytes=50 << 20
        ),
        name="reduce",
    )(gradients[0, 0], errors[0, 0], jnp.swapaxes(old_basis, 1, 2))
    residual, new_basis = pl.pallas_call(
        residual_kernel,
        out_shape=(
            jax.ShapeDtypeStruct((matrices, rows, cols), jnp.bfloat16),
            jax.ShapeDtypeStruct((matrices, rank, cols), f32),
        ),
        in_specs=[vmem] * 3,
        out_specs=(any_space,) * 2,
        scratch_shapes=[
            pltpu.VMEM((matrices, rows, cols), jnp.bfloat16),
            pltpu.SemaphoreType.DMA,
            pltpu.SemaphoreType.DMA,
        ],
        compiler_params=pltpu.CompilerParams(vmem_limit_bytes=24 << 20),
        name="residual",
    )(merged, factors, basis)
    return residual[None, None], jnp.swapaxes(new_basis, 1, 2)


def solution(mesh):
    in_specs = (P("dp", "outer", None, None, None), P("dp", "outer", None, None, None), P())
    out_specs = (P("dp", "outer", None, None, None), P())
    return jax.shard_map(shards, mesh=mesh, in_specs=in_specs, out_specs=out_specs, check_vma=False)
```

time: 52.7 us -> 43.5 us (0.83)
  local copies, waits for them, and re-layouts: 4.89 us -> 0 us
  Pallas kernels: 47 us -> 42.8 us
    unnamed x6 -> x0, local copies, waits for them, and re-layouts: 4.89 us -> none
    pallas_call x1, Pallas kernels: 44.8 us -> 40.7 us  [shards(): pl.pallas_call(reduce_kernel, out_shape=(pltpu.VMEM((matrices, rows, cols...]
where the time goes in v2:
time: 43.5 us; the launch traced here: 43.4 us
  Pallas kernels  42.8 us (98%)
  between operations  0.64 us (1%)
    pallas_call x1, Pallas kernels, shards(): pl.pallas_call(reduce_kernel, out_shape=(pltpu.VMEM((matrices, rows, cols...  40.7 us
    pallas_call x1, Pallas kernels, shards(): pl.pallas_call(residual_kernel, out_shape=(jax.ShapeDtypeStruct((matrices...  2.11 us

profile of v2, /device:TPU:1, one launch (start us, length us, event | category | flops | bytes accessed | tf_op | source)
XLA Modules:
  0.0 43.4 jit_solution(5006292313927838288)
XLA Ops:
  0.6 40.7 %reduce.1 = (f32[2,1024,896]{2,1,0:T(8,128)S(1)}, bf16[2,1024,128]{2,1,0:T(8,128)(2,1)S(1)}, f32[2,8,896]{2,1,0:T(8,128)S(1)}) custom-call(bf16[2,1024,896]{2,1,0:T(8,128)(2,1)} %bitcast.5, bf16[2,1024,896]{2,1,0:T(8,128)(2,1)} %bitcast.6, f32[2,8,896]{2,1,0:T(8,128)} %bitcast.7), custom_call_target="tpu_custom_call" | custom-call | tf_op jit(solution)/shard_map/reduce/pallas_call | solution.py:249
  41.3 2.1 %residual.1 = (bf16[2,1024,896]{2,1,0:T(8,128)(2,1)}, f32[2,8,896]{2,1,0:T(8,128)}) custom-call(f32[2,1024,896]{2,1,0:T(8,128)S(1)} %get-tuple-element.7.merged, bf16[2,1024,128]{2,1,0:T(8,128)(2,1)S(1)} %get-tuple-element.8.factors, f32[2,8,896]{2,1,0:T(8,128)S(1)} %get-tuple-element.9.basis), custom_call_target="tpu_custom_call" | custom-call | tf_op jit(solution)/shard_map/residual/pallas_call | solution.py:276

commit v3 on v2

--- a/solution.py
+++ b/solution.py
@@ -17,6 +17,7 @@
 BLOCK = 256
 LOAD = 512
 FAR = 5
+HALF, FIRST, SECOND = 2, 2, 0
 
 
 def ring(d, n):
@@ -60,21 +61,9 @@
     dp, y = lax.axis_index("dp"), lax.axis_index("outer")
     x, z, c = lax.div(dp, NZ * NC), lax.rem(lax.div(dp, NC), NZ), lax.rem(dp, NC)
     own, other = c, 1 - c
-    place_xy = x * NY + y
-    sender = place_xy * NC + c
-
-    here, across = [], []
-    for dx, dy in XY_OFFSETS:
-        tx, ty = lax.rem(x + dx, NX), lax.rem(y + dy, NY)
-        index = tx * NY + ty
-        if dx or dy:
-            here.append((index, {"dp": (tx * NZ + z) * NC + own, "outer": ty}))
-        across.append((index, {"dp": (tx * NZ + z) * NC + other, "outer": ty}))
-    column = [{"dp": (x * NZ + lax.rem(z + d, NZ)) * NC + c, "outer": y} for d in Z_OFFSETS]
-    partners = [d for _, d in across[:4]] + column[:3] + [d for _, d in here + across[4:]] + column[3:]
-    barrier = pltpu.get_barrier_semaphore()
-    for device in partners:
-        pl.semaphore_signal(barrier, inc=1, device_id=device, device_id_type=MESH)
+    sender = (x * NY + y) * NC + c
+    half, column_of_half = lax.div(x, HALF), lax.rem(x, HALF)
+    mine = column_of_half * NY + y
 
     q_copy = pltpu.make_async_copy(q_hbm, qv, q_sem)
     q_copy.start()
@@ -85,9 +74,21 @@
             pair = []
             for a, (src, dst) in enumerate(((g_hbm, gv), (e_hbm, ev))):
                 copy = pltpu.make_async_copy(src.at[m, at], dst.at[m, at], in_sem.at[n, i, a])
-                copy.start(priority=n)
+                copy.start(priority=1)
                 pair.append(copy)
             loads.append((n, m, i, pair))
+
+    here, across = [], []
+    for dx, dy in XY_OFFSETS:
+        tx, ty = lax.rem(x + dx, NX), lax.rem(y + dy, NY)
+        if dx or dy:
+            here.append({"dp": (tx * NZ + z) * NC + own, "outer": ty})
+        across.append({"dp": (tx * NZ + z) * NC + other, "outer": ty})
+    column = [{"dp": (x * NZ + lax.rem(z + d, NZ)) * NC + c, "outer": y} for d in Z_OFFSETS]
+    partners = across[:4] + column[:3] + here + across[4:] + column[3:]
+    barrier = pltpu.get_barrier_semaphore()
+    for device in partners:
+        pl.semaphore_signal(barrier, inc=1, device_id=device, device_id_type=MESH)
 
     def wait_all(ref, sem):
         pltpu.make_async_copy(ref, ref, sem).wait()
@@ -98,14 +99,29 @@
             device_id=device, device_id_type=MESH,
         ).start()
 
-    def scatter_across(send, m, slot, k):
-        for index, device in across:
+    def targets(core, first):
+        for dy in (2, 1, 3, 0):
+            for i in range(HALF):
+                ty = lax.rem(y + dy, NY)
+                yield dy, i, i * NY + ty, {"dp": ((first + i) * NZ + z) * NC + core, "outer": ty}
+
+    def scatter_across(send, m, slot, k, first):
+        for _, _, index, device in targets(other, first):
             remote(send.at[m, index], slot.at[sender], k, k, device)
 
-    def scatter_here(send, m, slot, k):
-        for index, device in here:
-            remote(send.at[m, index], slot.at[sender], k, k, device)
-        pltpu.make_async_copy(send.at[m, place_xy], slot.at[sender], recv_sem.at[k]).start()
+    def scatter_here(send, m, slot, k, first):
+        for dy, i, index, device in targets(own, first):
+            if dy:
+                remote(send.at[m, index], slot.at[sender], k, k, device)
+                continue
+
+            @pl.when(x == first + i)
+            def _():
+                pltpu.make_async_copy(send.at[m, index], slot.at[sender], recv_sem.at[k]).start()
+
+            @pl.when(x != first + i)
+            def _():
+                remote(send.at[m, index], slot.at[sender], k, k, device)
 
     def exchange(slot, part, zslot, k):
         wait_all(slot, recv_sem.at[k])
@@ -117,21 +133,19 @@
     def spread(zslot, final, gather, m, k):
         wait_all(zslot, recv_sem.at[k + 1])
         final[...] = tree_sum([zslot[i] for i in range(NZ)]) * (1.0 / REPLICAS)
-        for _, device in here[:FAR]:
-            remote(final, gather.at[m, place_xy], k + 2, k + 2, device)
-        for _, device in across:
-            remote(final, gather.at[m, place_xy], k + 2, k + 3, device)
-        for _, device in here[FAR:]:
-            remote(final, gather.at[m, place_xy], k + 2, k + 2, device)
-        pltpu.make_async_copy(final, gather.at[m, place_xy], recv_sem.at[k + 2]).start()
+        for device in here[:FAR]:
+            remote(final, gather.at[m, mine], k + 2, k + 2, device)
+        for device in across:
+            remote(final, gather.at[m, mine], k + 2, k + 3, device)
+        for device in here[FAR:]:
+            remote(final, gather.at[m, mine], k + 2, k + 2, device)
+        pltpu.make_async_copy(final, gather.at[m, mine], recv_sem.at[k + 2]).start()
 
     def assembled(gather, m, blocks):
-        tiles = [jnp.concatenate([gather[m, b], gather[m, 8 + b]], axis=0) for b in range(blocks)]
-        return jnp.concatenate(tiles, axis=1)
+        return jnp.concatenate([gather[m, b] for b in range(blocks)], axis=1)
 
     def place(send, m, b, tile):
-        send[m, b] = tile[0:4]
-        send[m, 8 + b] = tile[4:8]
+        send[m, b] = tile
 
     contract_last = (((1,), (1,)), ((), ()))
     q_copy.wait()
@@ -146,16 +160,19 @@
         )
         for b in range(LOAD // 128):
             place(send1, m, i * (LOAD // 128) + b, left[:, b * 128 : (b + 1) * 128])
-        if n == 1 and i == per - 2:
-            pl.semaphore_wait(barrier, len(partners))
-            scatter_across(send1, other, slot1, 0)
-    scatter_here(send1, own, slot1, 0)
+    pl.semaphore_wait(barrier, len(partners))
+    scatter_across(send1, other, slot1, 0, FIRST)
+    scatter_here(send1, own, slot1, 0, FIRST)
     for n in range(2):
         for i in range(rows // BLOCK):
             at = pl.ds(i * BLOCK, BLOCK)
             merged[n, at] = gv[n, at].astype(jnp.float32) + ev[n, at].astype(jnp.float32)
-    exchange(slot1, part1, zslot1, 0)
-    spread(zslot1, final1, gather1, own, 0)
+
+    @pl.when(half == FIRST // HALF)
+    def _():
+        exchange(slot1, part1, zslot1, 0)
+        spread(zslot1, final1, gather1, own, 0)
+
 
     def right(m):
         mean = assembled(gather1, m, rows // 128)
@@ -171,17 +188,17 @@
         return mean
 
     wait_all(gather1.at[own], recv_sem.at[2])
+    wait_all(gather1.at[other], recv_sem.at[3])
     mean_own = right(own)
-    scatter_across(send2, own, slot2, 4)
-    wait_all(gather1.at[other], recv_sem.at[3])
     mean_other = right(other)
-    scatter_here(send2, other, slot2, 4)
+    scatter_across(send2, own, slot2, 4, SECOND)
+    scatter_here(send2, other, slot2, 4, SECOND)
 
     row_of = lax.broadcasted_iota(jnp.int32, (8, 1), 0)
     eye = (
         lax.broadcasted_iota(jnp.int32, (8, 8), 0) == lax.broadcasted_iota(jnp.int32, (8, 8), 1)
     ).astype(jnp.float32)
-    inverses = []
+    solutions = []
     for m, mean in ((own, mean_own), (other, mean_other)):
         gram = lax.dot_general(mean, mean, contract_last, precision=HIGHEST, preferred_element_type=jnp.float32)
         gram = gram + EPSILON * eye
@@ -195,23 +212,38 @@
             inverse = jnp.where(row_of == k, first, inverse - below * first)
             first = solved[k : k + 1, :] / pivot
             solved = jnp.where(row_of == k, first, solved - below * first)
-        inverses.append((m, inverse))
+        solutions.append((m, inverse, solved))
+
+    @pl.when(half == SECOND // HALF)
+    def _():
+        exchange(slot2, part2, zslot2, 4)
+
+    for m, _, solved in solutions:
         o1, o2, o3 = split3(solved)
         wide = jnp.concatenate([o1, o1, o2, o2, o1, o3, jnp.zeros((80, rows), jnp.float32)], axis=0)
         factors[m] = jnp.transpose(wide).astype(jnp.bfloat16)
 
-    exchange(slot2, part2, zslot2, 4)
-    spread(zslot2, final2, gather2, other, 4)
+    @pl.when(half == SECOND // HALF)
+    def _():
+        spread(zslot2, final2, gather2, other, 4)
+
     wait_all(gather2.at[other], recv_sem.at[6])
     wait_all(gather2.at[own], recv_sem.at[7])
-    for m, inverse in inverses:
+    for m, inverse, _ in solutions:
         raw = assembled(gather2, m, cols // 128)
         basis[m] = tree_sum([inverse[:, t : t + 1] * raw[t : t + 1, :] for t in range(8)])
 
-    for k in (0, 4):
-        wait_all(slot1.at[pl.ds(0, PLANE - 1)], send_sem.at[k])
-        wait_all(zslot1.at[pl.ds(0, NZ - 1)], send_sem.at[k + 1])
-        wait_all(slot1.at[pl.ds(0, PLANE - 1)], send_sem.at[k + 2])
+    for k, first in ((0, FIRST), (4, SECOND)):
+
+        @pl.when(half == first // HALF)
+        def _():
+            wait_all(slot1.at[pl.ds(0, NC * HALF * NY - 1)], send_sem.at[k])
+            wait_all(zslot1.at[pl.ds(0, NZ - 1)], send_sem.at[k + 1])
+            wait_all(slot1.at[pl.ds(0, PLANE - 1)], send_sem.at[k + 2])
+
+        @pl.when(half != first // HALF)
+        def _():
+            wait_all(slot1.at[pl.ds(0, NC * HALF * NY)], send_sem.at[k])
 
 
 def residual_kernel(merged, factors, basis, out_hbm, basis_hbm, buffer, out_sem, basis_sem):
@@ -239,12 +271,12 @@
     vmem = pl.BlockSpec(memory_space=pltpu.VMEM)
     f32 = jnp.float32
     stage = [
-        pltpu.VMEM((matrices, 16, 4, 128), f32),
-        pltpu.VMEM((PLANE, 4, 128), f32),
-        pltpu.VMEM((4, 128), f32),
-        pltpu.VMEM((NZ, 4, 128), f32),
-        pltpu.VMEM((4, 128), f32),
-        pltpu.VMEM((matrices, 16, 4, 128), f32),
+        pltpu.VMEM((matrices, HALF * NY, 8, 128), f32),
+        pltpu.VMEM((PLANE, 8, 128), f32),
+        pltpu.VMEM((8, 128), f32),
+        pltpu.VMEM((NZ, 8, 128), f32),
+        pltpu.VMEM((8, 128), f32),
+        pltpu.VMEM((matrices, HALF * NY, 8, 128), f32),
     ]
     merged, factors, basis = pl.pallas_call(
         reduce_kernel,

time: 43.5 us -> 41.7 us (0.959)
  Pallas kernels: 42.8 us -> 41 us
    pallas_call x1, Pallas kernels: 40.7 us -> 38.9 us  [shards(): pl.pallas_call(reduce_kernel, out_shape=(pltpu.VMEM((matrices, rows, cols...]
where the time goes in v3:
time: 41.7 us
  Pallas kernels  41 us (98%)
  between operations  0.64 us (2%)
    pallas_call x1, Pallas kernels, shards(): pl.pallas_call(reduce_kernel, out_shape=(pltpu.VMEM((matrices, rows, cols...  38.9 us
    pallas_call x1, Pallas kernels, shards(): pl.pallas_call(residual_kernel, out_shape=(jax.ShapeDtypeStruct((matrices...  2.12 us

profile of v3, /device:TPU:1, one launch (start us, length us, event | category | flops | bytes accessed | tf_op | source)
XLA Modules:
  0.0 41.7 jit_solution(4527905603721467533)
XLA Ops:
  0.6 38.9 %reduce.1 = (f32[2,1024,896]{2,1,0:T(8,128)S(1)}, bf16[2,1024,128]{2,1,0:T(8,128)(2,1)S(1)}, f32[2,8,896]{2,1,0:T(8,128)S(1)}) custom-call(bf16[2,1024,896]{2,1,0:T(8,128)(2,1)} %bitcast.5, bf16[2,1024,896]{2,1,0:T(8,128)(2,1)} %bitcast.6, f32[2,8,896]{2,1,0:T(8,128)} %bitcast.7), custom_call_target="tpu_custom_call" | custom-call | tf_op jit(solution)/shard_map/reduce/pallas_call | solution.py:281
  39.5 2.1 %residual.1 = (bf16[2,1024,896]{2,1,0:T(8,128)(2,1)}, f32[2,8,896]{2,1,0:T(8,128)}) custom-call(f32[2,1024,896]{2,1,0:T(8,128)S(1)} %get-tuple-element.7.merged, bf16[2,1024,128]{2,1,0:T(8,128)(2,1)S(1)} %get-tuple-element.8.factors, f32[2,8,896]{2,1,0:T(8,128)S(1)} %get-tuple-element.9.basis), custom_call_target="tpu_custom_call" | custom-call | tf_op jit(solution)/shard_map/residual/pallas_call | solution.py:308

commit v4 on v3

--- a/solution.py
+++ b/solution.py
@@ -16,7 +16,7 @@
 REPLICAS = PLANE * NZ
 BLOCK = 256
 LOAD = 512
-FAR = 5
+OUT = 128
 HALF, FIRST, SECOND = 2, 2, 0
 
 
@@ -133,12 +133,10 @@
     def spread(zslot, final, gather, m, k):
         wait_all(zslot, recv_sem.at[k + 1])
         final[...] = tree_sum([zslot[i] for i in range(NZ)]) * (1.0 / REPLICAS)
-        for device in here[:FAR]:
+        for device in here:
             remote(final, gather.at[m, mine], k + 2, k + 2, device)
         for device in across:
             remote(final, gather.at[m, mine], k + 2, k + 3, device)
-        for device in here[FAR:]:
-            remote(final, gather.at[m, mine], k + 2, k + 2, device)
         pltpu.make_async_copy(final, gather.at[m, mine], recv_sem.at[k + 2]).start()
 
     def assembled(gather, m, blocks):
@@ -255,11 +253,11 @@
         terms = jnp.concatenate(
             [b1, b2, b1, b2, b3, b1, jnp.zeros((80, cols), jnp.float32)], axis=0
         ).astype(jnp.bfloat16)
-        for i in range(rows // BLOCK):
-            at = pl.ds(i * BLOCK, BLOCK)
+        for i in range(rows // OUT):
+            at = pl.ds(i * OUT, OUT)
             update = jnp.dot(factors[m, at], terms, preferred_element_type=jnp.float32)
             buffer[m, at] = (merged[m, at] - update).astype(jnp.bfloat16)
-            pltpu.make_async_copy(buffer.at[m, at], out_hbm.at[m, at], out_sem).start()
+            pltpu.make_async_copy(buffer.at[m, at], out_hbm.at[m, at], out_sem).start(priority=i % 2)
     pltpu.make_async_copy(buffer, out_hbm, out_sem).wait()
     basis_copy.wait()
 

time: 41.7 us -> 41.4 us (level)
  no operation moved by 1% of the time
where the time goes in v4:
time: 41.4 us; the launch traced here: 41.3 us
  Pallas kernels  40.7 us (98%)
  between operations  0.64 us (2%)
    pallas_call x1, Pallas kernels, shards(): pl.pallas_call(reduce_kernel, out_shape=(pltpu.VMEM((matrices, rows, cols...  38.7 us
    pallas_call x1, Pallas kernels, shards(): pl.pallas_call(residual_kernel, out_shape=(jax.ShapeDtypeStruct((matrices...  2.05 us

profile of v4, /device:TPU:1, one launch (start us, length us, event | category | flops | bytes accessed | tf_op | source)
XLA Modules:
  0.0 41.3 jit_solution(16225305206649131444)
XLA Ops:
  0.6 38.7 %reduce.1 = (f32[2,1024,896]{2,1,0:T(8,128)S(1)}, bf16[2,1024,128]{2,1,0:T(8,128)(2,1)S(1)}, f32[2,8,896]{2,1,0:T(8,128)S(1)}) custom-call(bf16[2,1024,896]{2,1,0:T(8,128)(2,1)} %bitcast.5, bf16[2,1024,896]{2,1,0:T(8,128)(2,1)} %bitcast.6, f32[2,8,896]{2,1,0:T(8,128)} %bitcast.7), custom_call_target="tpu_custom_call" | custom-call | tf_op jit(solution)/shard_map/reduce/pallas_call | solution.py:279
  39.3 2.1 %residual.1 = (bf16[2,1024,896]{2,1,0:T(8,128)(2,1)}, f32[2,8,896]{2,1,0:T(8,128)}) custom-call(f32[2,1024,896]{2,1,0:T(8,128)S(1)} %get-tuple-element.7.merged, bf16[2,1024,128]{2,1,0:T(8,128)(2,1)S(1)} %get-tuple-element.8.factors, f32[2,8,896]{2,1,0:T(8,128)S(1)} %get-tuple-element.9.basis), custom_call_target="tpu_custom_call" | custom-call | tf_op jit(solution)/shard_map/residual/pallas_call | solution.py:306

commit v5 on v4

--- a/solution.py
+++ b/solution.py
@@ -225,9 +225,8 @@
     def _():
         spread(zslot2, final2, gather2, other, 4)
 
-    wait_all(gather2.at[other], recv_sem.at[6])
-    wait_all(gather2.at[own], recv_sem.at[7])
-    for m, inverse, _ in solutions:
+    for (m, inverse, _), group in ((solutions[1], 6), (solutions[0], 7)):
+        wait_all(gather2.at[m], recv_sem.at[group])
         raw = assembled(gather2, m, cols // 128)
         basis[m] = tree_sum([inverse[:, t : t + 1] * raw[t : t + 1, :] for t in range(8)])
 

time: 41.4 us -> 41.4 us (level)
  no operation moved by 1% of the time
where the time goes in v5:
time: 41.4 us; the launch traced here: 41.3 us
  Pallas kernels  40.7 us (98%)
  between operations  0.64 us (2%)
    pallas_call x1, Pallas kernels, shards(): pl.pallas_call(reduce_kernel, out_shape=(pltpu.VMEM((matrices, rows, cols...  38.6 us
    pallas_call x1, Pallas kernels, shards(): pl.pallas_call(residual_kernel, out_shape=(jax.ShapeDtypeStruct((matrices...  2.05 us

profile of v5, /device:TPU:1, one launch (start us, length us, event | category | flops | bytes accessed | tf_op | source)
XLA Modules:
  0.0 41.3 jit_solution(8992872015584525694)
XLA Ops:
  0.6 38.6 %reduce.1 = (f32[2,1024,896]{2,1,0:T(8,128)S(1)}, bf16[2,1024,128]{2,1,0:T(8,128)(2,1)S(1)}, f32[2,8,896]{2,1,0:T(8,128)S(1)}) custom-call(bf16[2,1024,896]{2,1,0:T(8,128)(2,1)} %bitcast.5, bf16[2,1024,896]{2,1,0:T(8,128)(2,1)} %bitcast.6, f32[2,8,896]{2,1,0:T(8,128)} %bitcast.7), custom_call_target="tpu_custom_call" | custom-call | tf_op jit(solution)/shard_map/reduce/pallas_call | solution.py:278
  39.3 2.0 %residual.1 = (bf16[2,1024,896]{2,1,0:T(8,128)(2,1)}, f32[2,8,896]{2,1,0:T(8,128)}) custom-call(f32[2,1024,896]{2,1,0:T(8,128)S(1)} %get-tuple-element.7.merged, bf16[2,1024,128]{2,1,0:T(8,128)(2,1)S(1)} %get-tuple-element.8.factors, f32[2,8,896]{2,1,0:T(8,128)S(1)} %get-tuple-element.9.basis), custom_call_target="tpu_custom_call" | custom-call | tf_op jit(solution)/shard_map/residual/pallas_call | solution.py:305

commit v6 on v5

--- a/solution.py
+++ b/solution.py
@@ -147,17 +147,28 @@
 
     contract_last = (((1,), (1,)), ((), ()))
     q_copy.wait()
-    q_terms = [stacked(qv[m]) for m in (other, own)]
+    q_terms = []
+    for m in (other, own):
+        wide = jnp.concatenate([*split3(qv[m]), jnp.zeros((104, cols), jnp.float32)], axis=0)
+        q_terms.append(jnp.transpose(wide).astype(jnp.bfloat16))
+
+    def finish(m, i, product):
+        left = fold(jnp.transpose(product))
+        for b in range(LOAD // 128):
+            place(send1, m, i * (LOAD // 128) + b, left[:, b * 128 : (b + 1) * 128])
+
+    pending = None
     for n, m, i, pair in loads:
         for copy in pair:
             copy.wait()
         at = pl.ds(i * LOAD, LOAD)
-        left = fold(
-            lax.dot_general(q_terms[n], gv[m, at], contract_last, preferred_element_type=jnp.float32)
-            + lax.dot_general(q_terms[n], ev[m, at], contract_last, preferred_element_type=jnp.float32)
+        product = jnp.dot(gv[m, at], q_terms[n], preferred_element_type=jnp.float32) + jnp.dot(
+            ev[m, at], q_terms[n], preferred_element_type=jnp.float32
         )
-        for b in range(LOAD // 128):
-            place(send1, m, i * (LOAD // 128) + b, left[:, b * 128 : (b + 1) * 128])
+        if pending is not None:
+            finish(*pending)
+        pending = (m, i, product)
+    finish(*pending)
     pl.semaphore_wait(barrier, len(partners))
     scatter_across(send1, other, slot1, 0, FIRST)
     scatter_here(send1, own, slot1, 0, FIRST)

time: 41.4 us -> 41.4 us (level)
  no operation moved by 1% of the time
where the time goes in v6:
time: 41.4 us; the launch traced here: 41.3 us
  Pallas kernels  40.6 us (98%)
  between operations  0.64 us (2%)
    pallas_call x1, Pallas kernels, shards(): pl.pallas_call(reduce_kernel, out_shape=(pltpu.VMEM((matrices, rows, cols...  38.6 us
    pallas_call x1, Pallas kernels, shards(): pl.pallas_call(residual_kernel, out_shape=(jax.ShapeDtypeStruct((matrices...  2.05 us

profile of v6, /device:TPU:1, one launch (start us, length us, event | category | flops | bytes accessed | tf_op | source)
XLA Modules:
  0.0 41.3 jit_solution(8494878334565847646)
XLA Ops:
  0.6 38.6 %reduce.1 = (f32[2,1024,896]{2,1,0:T(8,128)S(1)}, bf16[2,1024,128]{2,1,0:T(8,128)(2,1)S(1)}, f32[2,8,896]{2,1,0:T(8,128)S(1)}) custom-call(bf16[2,1024,896]{2,1,0:T(8,128)(2,1)} %bitcast.5, bf16[2,1024,896]{2,1,0:T(8,128)(2,1)} %bitcast.6, f32[2,8,896]{2,1,0:T(8,128)} %bitcast.7), custom_call_target="tpu_custom_call" | custom-call | tf_op jit(solution)/shard_map/reduce/pallas_call | solution.py:289
  39.2 2.1 %residual.1 = (bf16[2,1024,896]{2,1,0:T(8,128)(2,1)}, f32[2,8,896]{2,1,0:T(8,128)}) custom-call(f32[2,1024,896]{2,1,0:T(8,128)S(1)} %get-tuple-element.7.merged, bf16[2,1024,128]{2,1,0:T(8,128)(2,1)S(1)} %get-tuple-element.8.factors, f32[2,8,896]{2,1,0:T(8,128)S(1)} %get-tuple-element.9.basis), custom_call_target="tpu_custom_call" | custom-call | tf_op jit(solution)/shard_map/residual/pallas_call | solution.py:316
